TPU v7x, 128 devices: a whole 4x4x4 slice. The times are simulated.
128 devices in a mesh: dp: 16 (over y_hi, z, core), seq: 8 (over y_lo, x).
Axes of the slice: x: 4, y: 4 (y_hi: 2, y_lo: 2; y = y_hi * 2 + y_lo), z: 4, core: 2. Of those that a mesh axis runs over, the one named last changes fastest.
Arguments:
- packed_bases: int32 [16, 2048], P('dp', 'seq'), may hold values from 0 to 1073741823
- rc_flags: int32 [16], P('dp'), may hold values 0 or 1
- shifts: int32 [16], P('dp'), may hold values from -3 to 3
- cotangent: bfloat16 [16, 15360, 608], P('dp', 'seq'), may hold values from -0.015625 to 0.015625
- stem_weight: bfloat16 [15, 4, 512], replicated, may hold values from -0.75 to 0.75
- pool_gain: float32 [512], replicated, may hold values from 0.5 to 8
- tower_weight: bfloat16 [608, 5, 512], replicated, may hold values from -0.125 to 0.125
Outputs:
- response: bfloat16 [16, 15360, 608], P('dp', 'seq')
- stem_grad: float32 [15, 4, 512], replicated
- gain_grad: float32 [512], replicated
- tower_grad: float32 [608, 5, 512], P('dp')
All inputs are finite; a program needn't handle non-finite values. No bound on the sum of `rc_flags` on one device may be relied on, other than what follows from the above.
Results may differ from a plain program's by a relative error of at most 0.0075.
Values may be sent and summed in bfloat16 or wider, within the bound.
A program may use at most 192 MiB of HBM per device.

v0:
```python
import functools
import jax
import jax.numpy as jnp
from jax import lax
from jax.experimental import pallas as pl
from jax.experimental.pallas import tpu as pltpu
from jax.sharding import PartitionSpec as P

F32, BF16, I32 = jnp.float32, jnp.bfloat16, jnp.int32
C1, F2, K1, K2 = 512, 608, 15, 5
ROWS = 1920
WIDE = 2048
KF = 3072
UNIT = 768
SEQ = 8
CH = 256


def dot(a, b):
    return lax.dot_general(a, b, (((1,), (0,)), ((), ())), preferred_element_type=F32)


def dot_nt(a, b):
    return lax.dot_general(a, b, (((1,), (1,)), ((), ())), preferred_element_type=F32)


def prep_stem_weight(sw_ref, sw_f, wcat, gain, gain_b):
    sw_f[60:64, 0:C1] = jnp.zeros((4, C1), F32)
    sw_f[0:4, C1:] = jnp.zeros((4, C1), F32)
    for s in range(K1):
        v = sw_ref[s].astype(F32)
        sw_f[4 * s : 4 * s + 4, 0:C1] = v
        sw_f[4 * s + 4 : 4 * s + 8, C1:] = v
    wcat[...] = sw_f[...].T.astype(BF16)
    gain_b[...] = jnp.broadcast_to(gain[...], (128, C1)).T


def prep_tower_weight(w5, wt):
    flat = w5.reshape(K2 * F2, C1)

    def block(i, _):
        r0 = pl.multiple_of(i * 128, 128)
        wt[:, pl.ds(r0, 128)] = flat[pl.ds(r0, 128), :].T
        return 0

    lax.fori_loop(0, (K2 * F2) // 128, block, 0)
    tail = K2 * F2 - (K2 * F2) // 128 * 128
    v = jnp.concatenate([flat[K2 * F2 - tail :, :], jnp.zeros((128 - tail, C1), BF16)], axis=0)
    wt[:, KF - 128 :] = v.T


def prep_cot(cot_v, halo, seq, gt):
    lane = lax.broadcasted_iota(I32, (16, 128), 1)

    def rows(i, _):
        r0 = pl.multiple_of(i * 16, 16)
        rs = pl.ds(r0, 16)
        nxt = jnp.where(seq < SEQ - 1, halo[1, rs, :].astype(F32), 0.0)
        prv = jnp.where(seq > 0, halo[0, rs, :].astype(F32), 0.0)
        rim = jnp.where(lane < 64, nxt, prv).astype(BF16)
        full = jnp.concatenate([cot_v[rs, :], rim], axis=1)
        for t in range(K2):
            s = 2 - t
            v = full if s == 0 else pltpu.roll(full, (-s) % WIDE, 1)
            gt[pl.ds(pl.multiple_of(t * F2 + r0, 16), 16), :] = v[:, 0:ROWS]
        return 0

    lax.fori_loop(0, F2 // 16, rows, 0)
    gt[K2 * F2 : KF, :] = jnp.zeros((KF - K2 * F2, ROWS), BF16)


def decode(words, rc, shift, seq, oh):
    take = jnp.where(rc == 1, SEQ - 1 - seq, seq)
    slot = lax.broadcasted_iota(I32, (SEQ, 1, CH), 0)
    w8 = words[...]
    own = jnp.sum(jnp.where(slot == take, w8, 0), axis=0)
    low = jnp.sum(jnp.where(slot == take - 1, w8, 0), axis=0)
    high = jnp.sum(jnp.where(slot == take + 1, w8, 0), axis=0)
    lane = lax.broadcasted_iota(I32, (1, 128), 1)
    rim = jnp.where(lane == 127, low[:, 128:256], jnp.where(lane == 0, high[:, 0:128], 0))
    row = jnp.broadcast_to(jnp.concatenate([own, rim], axis=1), (8, 384))
    after = jnp.where(rc == 1, pltpu.roll(row, 1, 1), pltpu.roll(row, 383, 1))
    sub = lax.broadcasted_iota(I32, (8, 384), 0)
    planes = (jnp.where(sub < 4, row, after) >> (8 * (sub & 3))) & 255
    planes = planes.astype(F32).astype(BF16)
    src = lax.broadcasted_iota(I32, (384, CH), 0)
    src = jnp.where(src == 383, -1, src)
    part = lax.broadcasted_iota(I32, (64, CH), 0)
    s = part >> 2
    want = jnp.where(rc == 1, 3 - (part & 3), part & 3)

    def chunk(i, _):
        u0 = pl.multiple_of(i * CH, CH)
        u = u0 + lax.broadcasted_iota(I32, (1, CH), 1)
        q = jnp.where(u < 1984, u, u - WIDE)
        b0 = 2 * q - 7 - shift
        j0 = (((b0 + 30) * 34953) >> 19) - 2
        i0 = b0 - 15 * j0
        at = jnp.where(rc == 1, 255 - j0, j0)
        sel = jnp.where(src == at, 1.0, 0.0).astype(BF16)
        got = dot(planes, sel).astype(I32)
        word_a = got[0:1] + (got[1:2] << 8) + (got[2:3] << 16) + (got[3:4] << 24)
        word_b = got[4:5] + (got[5:6] << 8) + (got[6:7] << 16) + (got[7:8] << 24)
        d = i0 + s
        late = d >= 15
        word = jnp.where(late, word_b, word_a)
        d = jnp.where(late, d - 15, d)
        d = jnp.where(rc == 1, 14 - d, d)
        where = 2 * ROWS * seq + b0 + s
        good = (where >= 0) & (where < 2 * ROWS * SEQ)
        hit = (((word >> (2 * d)) & 3) == want) & good
        oh[:, pl.ds(u0, CH)] = jnp.where(hit, 1.0, 0.0).astype(BF16)
        return 0

    lax.fori_loop(0, WIDE // CH, chunk, 0)


GELU_A = 0.7978845608028654
GELU_B = 0.044715


def forward(even, odd, gain):
    diff = even - odd
    weight = 0.5 * jnp.tanh((0.5 * gain) * diff) + 0.5
    x = odd + weight * diff
    x2 = x * x
    th = jnp.tanh(x * (GELU_A + (GELU_A * GELU_B) * x2))
    hx = 0.5 * x
    act = hx + hx * th
    return diff, weight, x2, th, hx, act


def slopes(gain, diff, weight, x2, th, hx):
    slope = weight - weight * weight
    dgelu = (0.5 + 0.5 * th) + hx * (1.0 - th * th) * (GELU_A + (3 * GELU_A * GELU_B) * x2)
    m1 = weight + gain * diff * slope
    m2 = diff * diff * slope
    return dgelu, m1, m2


def main_loop(oh, wcat, gain_b, seq, gt, wt, stem_s, ag_s, sg_s, act, gain_acc, stem_acc):
    gain_acc[...] = jnp.zeros_like(gain_acc)
    stem_acc[...] = jnp.zeros_like(stem_acc)

    def tile(n, lt, rows, rows2, u0, back):
        cols = slice(lt * 128, lt * 128 + 128)
        gain = gain_b[rows, :]
        diff, weight, x2, th, hx, a = forward(stem_s[rows, cols], stem_s[rows2, cols], gain)
        if not back:
            lane = lax.broadcasted_iota(I32, (16, 128), 1)
            out = ((lane < 64) & (seq == SEQ - 1)) | ((lane >= 64) & (seq == 0))
            a = jnp.where(out, 0.0, a)
        act[rows, pl.ds(pl.multiple_of(u0 + lt * 128, 128), 128)] = a.astype(BF16)
        if back:
            dgelu, m1, m2 = slopes(gain, diff, weight, x2, th, hx)
            pg = ag_s[rows, cols].astype(BF16).astype(F32) * dgelu
            dg = pg * m1
            sg_s[rows, cols] = dg.astype(BF16)
            sg_s[rows2, cols] = (pg - dg).astype(BF16)
            gain_acc[rows, :] += pg * m2

    def step(u0, width):
        us = pl.ds(u0, CH)
        stem_s[...] = dot(wcat[...], oh[:, us])
        ag_s[:, 0:width] = dot(wt[...], gt[:, pl.ds(u0, width)])

        def chunk(i, _):
            r0 = pl.multiple_of(i * 16, 16)
            rows = pl.ds(r0, 16)
            rows2 = pl.ds(pl.multiple_of(C1 + r0, 16), 16)
            for lt in range(2):
                tile(0, lt, rows, rows2, u0, lt * 128 < width)
            return 0

        lax.fori_loop(0, C1 // 16, chunk, 0, unroll=2)
        stem_acc[...] += dot_nt(sg_s[:, 0:width], oh[:, pl.ds(u0, width)])

    def group(g, _):
        step(pl.multiple_of(g * CH, CH), CH)
        return 0

    lax.fori_loop(0, 7, group, 0)
    step(7 * CH, 128)


def shift_act(act, xt):
    def rows(i, _):
        r0 = pl.multiple_of(i * 16, 16)
        full = act[pl.ds(r0, 16), :]
        for t in range(K2):
            s = t - 2
            v = full if s == 0 else pltpu.roll(full, (-s) % WIDE, 1)
            xt[pl.ds(pl.multiple_of(t * C1 + r0, 16), 16), :] = v[:, 0:ROWS]
        return 0

    lax.fori_loop(0, C1 // 16, rows, 0)


def tower_part(cot_v, xt, tg_s, unit_s):
    def tap(t, _):
        tg_s[...] = dot_nt(cot_v[...], xt[pl.ds(pl.multiple_of(t * C1, C1), C1), :])
        for d in range(16):
            for ct in range(4):
                piece = tg_s[38 * d : 38 * d + 38, ct * 128 : (ct + 1) * 128]
                unit_s[d, pl.ds(152 * t + 38 * ct, 38), :] = piece
        return 0

    lax.fori_loop(0, K2, tap, 0)
    for d in range(16):
        unit_s[d, 760:768, :] = jnp.zeros((8, 128), F32)


def response_step(xt, w5, resp_v, u0, width):
    taps = jnp.concatenate([w5[t] for t in range(K2)], axis=1)
    cols = pl.ds(u0, width)
    resp_v[:, cols] = dot(taps, xt[:, cols]).astype(BF16)


ORDER = ((0, 1, 2), (1, 2, 0), (2, 0, 1))
MESH = pl.DeviceIdType.MESH


def device_at(x, y, z, core):
    return ((y // 2) * 8 + z * 2 + core, (y % 2) * 4 + x)


def send(src, dst, ssem, rsem, to):
    return pltpu.make_async_remote_copy(
        src_ref=src, dst_ref=dst, send_sem=ssem, recv_sem=rsem, device_id=to, device_id_type=MESH
    )


def greet(me):
    barrier = pltpu.get_barrier_semaphore()
    x, y, z, core = me
    peers = []
    for dx in range(4):
        for dy in range(4):
            for dz in range(4):
                if (dx, dy, dz) != (0, 0, 0) and 0 in (dx, dy, dz):
                    peers.append(device_at((x + dx) % 4, (y + dy) % 4, (z + dz) % 4, core))
    for dz in range(4):
        peers.append(device_at(x, y, (z + dz) % 4, 1 - core))
    for peer in peers:
        pl.semaphore_signal(barrier, inc=1, device_id=peer, device_id_type=MESH)
    pl.semaphore_wait(barrier, len(peers))


def edge_copies(dp, seq, packed, cot_hbm, words, halo, ws, wr, hs, hr):
    out = []
    for d in range(1, SEQ):
        out.append(send(packed, words.at[seq], ws.at[d - 1], wr.at[d - 1], (dp, (seq + d) % SEQ)))
    out.append(send(cot_hbm.at[:, ROWS - 128 : ROWS], halo.at[0], hs.at[0], hr.at[0], (dp, (seq + 1) % SEQ)))
    out.append(send(cot_hbm.at[:, 0:128], halo.at[1], hs.at[1], hr.at[1], (dp, (seq + SEQ - 1) % SEQ)))
    return out


def pack_part(p, me, unit_s, own, oth):
    core = me[3]

    def piece(j, _):
        at = [None] * 3
        at[ORDER[p][0]], at[ORDER[p][1]], at[ORDER[p][2]] = j // 16, (j // 4) % 4, j % 4
        x, y, z = at
        unit = (y // 2) * 8 + z * 2
        rows = pl.ds(pl.multiple_of(p * 256 + x * 64 + (y % 2) * 32, 32), 32)
        own[p, j] = unit_s[unit + core, rows, :].astype(BF16)
        oth[p, j] = unit_s[unit + 1 - core, rows, :].astype(BF16)
        return 0

    lax.fori_loop(0, 64, piece, 0)


def pair_copy(p, me, oth, recv_d, ss, rs):
    x, y, z, core = me
    return send(oth.at[p], recv_d.at[p], ss.at[p], rs.at[p], device_at(x, y, z, 1 - core))


def pair_sum(p, own, recv_d):
    def piece(j, _):
        own[p, j] = (own[p, j].astype(F32) + recv_d[p, j].astype(F32)).astype(BF16)
        return 0

    lax.fori_loop(0, 64, piece, 0)


def ring_copies(p, me, own, recv_1, ss, rs):
    axis = ORDER[p][0]
    out = []
    for d in range(1, 4):
        to = list(me)
        to[axis] = (me[axis] + d) % 4
        src = own.at[p, pl.ds(to[axis] * 16, 16)]
        out.append(send(src, recv_1.at[p, d - 1], ss.at[p, d - 1], rs.at[p, d - 1], device_at(*to)))
    return out


def ring_sum(p, me, own, recv_1, buf_2):
    base = me[ORDER[p][0]] * 16

    def piece(j, _):
        total = own[p, base + j].astype(F32)
        for d in range(3):
            total = total + recv_1[p, d, j].astype(F32)
        buf_2[p, j] = total.astype(BF16)
        return 0

    lax.fori_loop(0, 16, piece, 0)


def plane_copies(p, me, buf_2, recv_2, ss, rs):
    b, c = ORDER[p][1], ORDER[p][2]
    out = []
    for e in range(1, 16):
        to = list(me)
        to[b] = (me[b] + e // 4) % 4
        to[c] = (me[c] + e % 4) % 4
        src = buf_2.at[p, to[b] * 4 + to[c]]
        out.append(send(src, recv_2.at[p, e - 1], ss.at[p, e - 1], rs.at[p, e - 1], device_at(*to)))
    return out


def plane_sum(p, me, buf_2, recv_2, fin):
    total = buf_2[p, me[ORDER[p][1]] * 4 + me[ORDER[p][2]]].astype(F32)
    for e in range(15):
        total = total + recv_2[p, e].astype(F32)
    fin[p] = total.astype(BF16)


def share_copies(dp, seq, fin, gath, ss, rs):
    return [
        send(fin, gath.at[seq], ss.at[d - 1], rs.at[d - 1], (dp, (seq + d) % SEQ)) for d in range(1, SEQ)
    ]


def place_tower(gath, flat, tower_ref):
    for s in range(SEQ):
        for p in range(3):
            r0 = p * 256 + (s % 4) * 64 + (s // 4) * 32
            flat[r0 : r0 + 32, :] = gath[s, p].astype(F32)
    for t in range(K2):
        for ct in range(4):
            j = 4 * t + ct
            tower_ref[t, :, ct * 128 : (ct + 1) * 128] = flat[38 * j : 38 * j + 38, :]


def pack_stem(stem_acc, gain_acc, stb):
    even = stem_acc[0:C1, :]
    odd = pltpu.roll(stem_acc[C1:, :], 60, 1) if False else jnp.concatenate(
        [stem_acc[C1:, 4:64], stem_acc[C1:, 0:4]], axis=1
    )
    lane = lax.broadcasted_iota(I32, (C1, 64), 1)
    gain = jnp.sum(gain_acc[...], axis=1, keepdims=True)
    both = jnp.where(lane < 60, even + odd, jnp.where(lane == 60, gain, 0.0)).T
    for i in range(16):
        stb[i] = both[(i % 8) * 8 : (i % 8) * 8 + 8, (i // 8) * 256 : (i // 8) * 256 + 256]


def stem_plane_copies(me, src_of, recv, slot_of, ss, rs):
    x, y, z, core = me
    out = []
    for e in range(1, 16):
        tx, ty = (x + e // 4) % 4, (y + e % 4) % 4
        out.append(
            send(src_of(tx * 4 + ty), recv.at[slot_of(e)], ss.at[e - 1], rs.at[e - 1], device_at(tx, ty, z, core))
        )
    return out


def stem_line_copies(me, piece, recv, ss, rs):
    x, y, z, core = me
    out = []
    for e in range(1, 8):
        to = device_at(x, y, (z + e // 2) % 4, (core + e % 2) % 2)
        out.append(send(piece, recv.at[z * 2 + core], ss.at[e - 1], rs.at[e - 1], to))
    return out


def place_stem(gath, stem_ref, gain_ref):
    for half in range(2):
        cols = slice(half * 256, half * 256 + 256)
        for s in range(K1):
            r = 4 * s
            stem_ref[s, :, cols] = gath[half * 8 + r // 8, r % 8 : r % 8 + 4, :]
        gain_ref[:, cols] = gath[half * 8 + 7, 4:5, :]


def start(copies):
    for c in copies:
        c.start()


def wait(copies):
    for c in copies:
        c.wait()


def whole_kernel(
    packed, rc_ref, sh_ref, cot_hbm, sw_ref, gain, w_hbm,
    resp_hbm, stem_ref, gain_ref, tower_ref,
    cot_v, w5, sw_f, wcat, gain_b, wt, gt, oh, act, xt,
    stem_s, ag_s, sg_s, gain_acc, stem_acc, resp_v, tg_s, unit_s,
    words, halo, own, oth, recv_d, recv_1, buf_2, recv_2, fin, gath, flat,
    stb, recv_a, piece_a, recv_b, piece_b, gath_a,
    sems, ws, wr, hs, hr, ds, dr, s1, r1, s2, r2, s3, r3, sa, ra, sb, rb, sg, rg,
):
    dp, seq = lax.axis_index("dp"), lax.axis_index("seq")
    x, y, z, core = seq % 4, (dp // 8) * 2 + seq // 4, (dp // 2) % 4, dp % 2
    me = (x, y, z, core)
    c1 = pltpu.make_async_copy(cot_hbm, cot_v, sems.at[0])
    c2 = pltpu.make_async_copy(w_hbm, w5, sems.at[1])
    c1.start()
    c2.start()
    greet(me)
    edges = edge_copies(dp, seq, packed, cot_hbm, words, halo, ws, wr, hs, hr)
    start(edges)
    words[seq] = packed[...]
    prep_stem_weight(sw_ref, sw_f, wcat, gain, gain_b)
    c2.wait()
    prep_tower_weight(w5, wt)
    wait(edges)
    decode(words, rc_ref[0], sh_ref[0], seq, oh)
    c1.wait()
    prep_cot(cot_v, halo, seq, gt)
    main_loop(oh, wcat, gain_b, seq, gt, wt, stem_s, ag_s, sg_s, act, gain_acc, stem_acc)
    pack_stem(stem_acc, gain_acc, stb)
    level_a = stem_plane_copies(me, lambda a: stb.at[a], recv_a, lambda e: e - 1, sa, ra)
    start(level_a)
    shift_act(act, xt)
    tower_part(cot_v, xt, tg_s, unit_s)
    pairs = []
    for p in range(3):
        pack_part(p, me, unit_s, own, oth)
        pairs.append(pair_copy(p, me, oth, recv_d, ds, dr))
        pairs[p].start()

    def resp(lo, hi):
        def group(g, _):
            response_step(xt, w5, resp_v, pl.multiple_of(g * CH, CH), CH)
            return 0

        lax.fori_loop(lo, hi, group, 0)

    resp(0, 2)
    rings = []
    for p in range(3):
        pairs[p].wait()
        pair_sum(p, own, recv_d)
        rings.append(ring_copies(p, me, own, recv_1, s1, r1))
        start(rings[p])
    wait(level_a)
    total = stb[x * 4 + y]
    for e in range(15):
        total = total + recv_a[e]
    piece_a[...] = total
    recv_b[z * 2 + core] = total
    level_b = stem_line_copies(me, piece_a, recv_b, sb, rb)
    start(level_b)
    resp(2, 5)
    planes = []
    wait(level_b)
    total = recv_b[0]
    for e in range(1, 8):
        total = total + recv_b[e]
    piece_b[...] = total
    gath_a[x * 4 + y] = total
    level_c = stem_plane_copies(me, lambda a: piece_b, gath_a, lambda e: x * 4 + y, sg, rg)
    start(level_c)
    resp(5, 7)
    response_step(xt, w5, resp_v, 7 * CH, 128)
    c3 = pltpu.make_async_copy(resp_v, resp_hbm, sems.at[0])
    c3.start()
    for p in range(3):
        wait(rings[p])
        ring_sum(p, me, own, recv_1, buf_2)
        planes.append(plane_copies(p, me, buf_2, recv_2, s2, r2))
        start(planes[p])
    wait(level_c)
    place_stem(gath_a, stem_ref, gain_ref)
    for p in range(3):
        wait(planes[p])
        plane_sum(p, me, buf_2, recv_2, fin)
    share = share_copies(dp, seq, fin, gath, s3, r3)
    start(share)
    gath[seq] = fin[...]
    c3.wait()
    wait(share)
    place_tower(gath, flat, tower_ref)


def scratch():
    V = pltpu.VMEM
    D = pltpu.SemaphoreType.DMA
    return [
        V((F2, ROWS), BF16),
        V((K2, F2, C1), BF16),
        V((64, 2 * C1), F32),
        V((2 * C1, 64), BF16),
        V((C1, 128), F32),
        V((C1, KF), BF16),
        V((KF, ROWS), BF16),
        V((64, WIDE), BF16),
        V((C1, WIDE), BF16),
        V((K2 * C1, ROWS), BF16),
        V((2 * C1, CH), F32),
        V((C1, CH), F32),
        V((2 * C1, CH), BF16),
        V((C1, 128), F32),
        V((2 * C1, 64), F32),
        V((F2, ROWS), BF16),
        V((F2, C1), F32),
        V((16, UNIT, 128), F32),
        V((SEQ, 1, 256), I32),
        V((2, F2, 128), BF16),
        V((3, 64, 32, 128), BF16),
        V((3, 64, 32, 128), BF16),
        V((3, 64, 32, 128), BF16),
        V((3, 3, 16, 32, 128), BF16),
        V((3, 16, 32, 128), BF16),
        V((3, 15, 32, 128), BF16),
        V((3, 32, 128), BF16),
        V((SEQ, 3, 32, 128), BF16),
        V((UNIT, 128), F32),
        V((16, 8, 256), F32),
        V((15, 8, 256), F32),
        V((8, 256), F32),
        V((8, 8, 256), F32),
        V((8, 256), F32),
        V((16, 8, 256), F32),
        D((2,)), D((7,)), D((7,)), D((2,)), D((2,)), D((3,)), D((3,)),
        D((3, 3)), D((3, 3)), D((3, 15)), D((3, 15)), D((7,)), D((7,)),
        D((15,)), D((15,)), D((7,)), D((7,)), D((15,)), D((15,)),
    ]


def shards(packed, rc_flags, shifts, cotangent, stem_weight, pool_gain, tower_weight):
    S = pl.BlockSpec(memory_space=pltpu.SMEM)
    VM = pl.BlockSpec(memory_space=pltpu.VMEM)
    A = pl.BlockSpec(memory_space=pl.ANY)
    resp, stem, gain, tower = pl.pallas_call(
        whole_kernel,
        out_shape=(
            jax.ShapeDtypeStruct((F2, ROWS), BF16),
            jax.ShapeDtypeStruct((K1, 4, C1), F32),
            jax.ShapeDtypeStruct((1, C1), F32),
            jax.ShapeDtypeStruct((K2, 38, C1), F32),
        ),
        in_specs=[VM, S, S, A, VM, VM, A],
        out_specs=(A, VM, VM, VM),
        scratch_shapes=scratch(),
        compiler_params=pltpu.CompilerParams(
            vmem_limit_bytes=62 * 1024 * 1024, collective_id=0, has_side_effects=True
        ),
    )(
        packed, rc_flags, shifts, cotangent[0].T, stem_weight, pool_gain[None],
        jnp.transpose(tower_weight, (1, 0, 2)),
    )
    return resp.T[None], stem, gain[0], jnp.transpose(tower, (1, 0, 2))


def solution(mesh):
    in_specs = (P("dp", "seq"), P("dp"), P("dp"), P("dp", "seq", None), P(), P(), P())
    out_specs = (P("dp", "seq", None), P(), P(), P("dp", None, None))
    return jax.shard_map(shards, mesh=mesh, in_specs=in_specs, out_specs=out_specs, check_vma=False)
```

profile of v0, /device:TPU:0, one launch (start us, length us, event | category | flops | bytes accessed | tf_op | source)
XLA Modules:
  0.0 94.8 jit_solution(13361278599104706827)
XLA Ops:
  1.9 87.6 %shard_map.102 = (bf16[608,1920]{1,0:T(8,128)(2,1)}, f32[15,4,512]{2,1,0:T(4,128)}, f32[1,512]{1,0:T(1,128)}, f32[5,38,512]{2,1,0:T(8,128)}) custom-call(s32[1,256]{1,0:T(1,128)} %packed.1, s32[1]{0:T(128)S(6)} %copy.15.rc_ref, s32[1]{0:T(128)S(6)} %copy.16.sh_ref, bf16[608,1920]{1,0:T(8,128)(2,1)} %bitcast.11, bf16[15,4,512]{2,1,0:T(4,128)(2,1)} %sw_ref.1, ...), custom_call_target="tpu_custom_call" | custom-call | tf_op jit(solution)/shard_map/pallas_call | solution.py:540
  89.5 0.0 copy-start.1
  89.5 0.0 copy-start.2
  89.5 0.0 copy-start
  89.5 3.3 %copy.17 = bf16[1,1920,608]{1,2,0:T(8,128)(2,1)} copy(bf16[1,1920,608]{1,2,0:T(8,128)(2,1)} %bitcast.12) | data formatting | bytes 4669440
  92.8 0.0 copy-done.1
  92.8 0.6 copy.18
  93.5 0.0 copy-done.2
  93.5 0.6 copy.19
  94.0 0.0 copy-done
  94.0 0.8 copy.20
Async XLA Ops:
  89.5 3.3 %copy-start.1 = (f32[15,4,512]{2,1,0:T(4,128)S(1)}, f32[15,4,512]{2,1,0:T(4,128)}, u32[]{:S(2)}) copy-start(f32[15,4,512]{2,1,0:T(4,128)} %get-tuple-element.17) | copy-start | bytes 368644
  89.5 4.0 %copy-start.2 = (f32[1,512]{1,0:T(1,128)S(1)}, f32[1,512]{1,0:T(1,128)}, u32[]{:S(2)}) copy-start(f32[1,512]{1,0:T(1,128)} %get-tuple-element.10) | copy-start | bytes 6148
  89.5 4.5 %copy-start = (f32[5,38,512]{2,1,0:T(8,128)S(1)}, f32[5,38,512]{2,1,0:T(8,128)}, u32[]{:S(2)}) copy-start(f32[5,38,512]{2,1,0:T(8,128)} %get-tuple-element.11) | copy-start | bytes 1167364
where the time goes:
time: 95 us; the launch traced here: 94.8 us
  Pallas kernels  87.6 us (92%)
  local copies, waits for them, and re-layouts  5.27 us (6%)
  between operations  1.96 us (2%)
    pallas_call x1, Pallas kernels, shards(): pl.pallas_call(whole_kernel, out_shape=(jax.ShapeDtypeStruct((F2, ROWS),...  87.6 us
    unnamed x10, local copies, waits for them, and re-layouts  5.27 us

commit v1 on v0

--- a/solution.py
+++ b/solution.py
@@ -25,14 +25,16 @@
 
 
 def prep_stem_weight(sw_ref, sw_f, wcat, gain, gain_b):
-    sw_f[60:64, 0:C1] = jnp.zeros((4, C1), F32)
-    sw_f[0:4, C1:] = jnp.zeros((4, C1), F32)
+    sw_f[60:68, :] = jnp.zeros((8, C1), F32)
     for s in range(K1):
-        v = sw_ref[s].astype(F32)
-        sw_f[4 * s : 4 * s + 4, 0:C1] = v
-        sw_f[4 * s + 4 : 4 * s + 8, C1:] = v
-    wcat[...] = sw_f[...].T.astype(BF16)
-    gain_b[...] = jnp.broadcast_to(gain[...], (128, C1)).T
+        v = sw_ref[s].astype(F32) * 0.25
+        sw_f[4 * s : 4 * s + 4, :] = v
+        sw_f[68 + 4 * s : 72 + 4 * s, :] = v
+    w = sw_f[...].T
+    lane = lax.broadcasted_iota(I32, (C1, 128), 1)
+    wcat[0:C1, :] = jnp.where(lane < 64, w, -w).astype(BF16)
+    wcat[C1:, :] = w.astype(BF16)
+    gain_b[...] = jnp.broadcast_to(gain[...], (128, C1)).T * 2.0
 
 
 def prep_tower_weight(w5, wt):
@@ -43,30 +45,40 @@
         wt[:, pl.ds(r0, 128)] = flat[pl.ds(r0, 128), :].T
         return 0
 
-    lax.fori_loop(0, (K2 * F2) // 128, block, 0)
+    lax.fori_loop(0, (K2 * F2) // 128, block, 0, unroll=True)
     tail = K2 * F2 - (K2 * F2) // 128 * 128
     v = jnp.concatenate([flat[K2 * F2 - tail :, :], jnp.zeros((128 - tail, C1), BF16)], axis=0)
     wt[:, KF - 128 :] = v.T
 
 
-def prep_cot(cot_v, halo, seq, gt):
-    lane = lax.broadcasted_iota(I32, (16, 128), 1)
-
+def prep_cot(cot_v, gt):
     def rows(i, _):
         r0 = pl.multiple_of(i * 16, 16)
-        rs = pl.ds(r0, 16)
+        full = cot_v[pl.ds(r0, 16), :]
+        for t in range(K2):
+            s = 2 - t
+            v = full if s == 0 else pltpu.roll(full, (-s) % ROWS, 1)
+            gt[pl.ds(pl.multiple_of(t * F2 + r0, 16), 16), :] = v
+        return 0
+
+    lax.fori_loop(0, F2 // 16, rows, 0, unroll=True)
+    gt[K2 * F2 : KF, :] = jnp.zeros((KF - K2 * F2, ROWS), BF16)
+
+
+def rim_cot(cot_v, halo, seq, gt):
+    lane = lax.broadcasted_iota(I32, (16, 128), 1)
+    for r in range(0, F2, 16):
+        rs = slice(r, r + 16)
         nxt = jnp.where(seq < SEQ - 1, halo[1, rs, :].astype(F32), 0.0)
         prv = jnp.where(seq > 0, halo[0, rs, :].astype(F32), 0.0)
         rim = jnp.where(lane < 64, nxt, prv).astype(BF16)
-        full = jnp.concatenate([cot_v[rs, :], rim], axis=1)
+        ring = jnp.concatenate([cot_v[rs, ROWS - 256 : ROWS], rim, cot_v[rs, 0:256]], axis=1)
         for t in range(K2):
             s = 2 - t
-            v = full if s == 0 else pltpu.roll(full, (-s) % WIDE, 1)
-            gt[pl.ds(pl.multiple_of(t * F2 + r0, 16), 16), :] = v[:, 0:ROWS]
-        return 0
-
-    lax.fori_loop(0, F2 // 16, rows, 0)
-    gt[K2 * F2 : KF, :] = jnp.zeros((KF - K2 * F2, ROWS), BF16)
+            if s != 0:
+                v = pltpu.roll(ring, (-s) % 640, 1)
+                gt[t * F2 + r : t * F2 + r + 16, ROWS - 128 : ROWS] = v[:, 128:256]
+                gt[t * F2 + r : t * F2 + r + 16, 0:128] = v[:, 384:512]
 
 
 def decode(words, rc, shift, seq, oh):
@@ -109,111 +121,104 @@
         where = 2 * ROWS * seq + b0 + s
         good = (where >= 0) & (where < 2 * ROWS * SEQ)
         hit = (((word >> (2 * d)) & 3) == want) & good
-        oh[:, pl.ds(u0, CH)] = jnp.where(hit, 1.0, 0.0).astype(BF16)
+        hot = jnp.where(hit, 1.0, 0.0).astype(BF16)
+        oh[0:64, pl.ds(u0, CH)] = hot
+        oh[64:128, pl.ds(u0, CH)] = hot
         return 0
 
-    lax.fori_loop(0, WIDE // CH, chunk, 0)
+    lax.fori_loop(0, WIDE // CH, chunk, 0, unroll=True)
 
 
 GELU_A = 0.7978845608028654
 GELU_B = 0.044715
 
 
-def forward(even, odd, gain):
-    diff = even - odd
-    weight = 0.5 * jnp.tanh((0.5 * gain) * diff) + 0.5
-    x = odd + weight * diff
-    x2 = x * x
-    th = jnp.tanh(x * (GELU_A + (GELU_A * GELU_B) * x2))
-    hx = 0.5 * x
-    act = hx + hx * th
-    return diff, weight, x2, th, hx, act
-
-
-def slopes(gain, diff, weight, x2, th, hx):
-    slope = weight - weight * weight
-    dgelu = (0.5 + 0.5 * th) + hx * (1.0 - th * th) * (GELU_A + (3 * GELU_A * GELU_B) * x2)
-    m1 = weight + gain * diff * slope
-    m2 = diff * diff * slope
-    return dgelu, m1, m2
-
-
-def main_loop(oh, wcat, gain_b, seq, gt, wt, stem_s, ag_s, sg_s, act, gain_acc, stem_acc):
-    gain_acc[...] = jnp.zeros_like(gain_acc)
-    stem_acc[...] = jnp.zeros_like(stem_acc)
-
-    def tile(n, lt, rows, rows2, u0, back):
-        cols = slice(lt * 128, lt * 128 + 128)
-        gain = gain_b[rows, :]
-        diff, weight, x2, th, hx, a = forward(stem_s[rows, cols], stem_s[rows2, cols], gain)
-        if not back:
-            lane = lax.broadcasted_iota(I32, (16, 128), 1)
-            out = ((lane < 64) & (seq == SEQ - 1)) | ((lane >= 64) & (seq == 0))
-            a = jnp.where(out, 0.0, a)
-        act[rows, pl.ds(pl.multiple_of(u0 + lt * 128, 128), 128)] = a.astype(BF16)
-        if back:
-            dgelu, m1, m2 = slopes(gain, diff, weight, x2, th, hx)
-            pg = ag_s[rows, cols].astype(BF16).astype(F32) * dgelu
-            dg = pg * m1
-            sg_s[rows, cols] = dg.astype(BF16)
-            sg_s[rows2, cols] = (pg - dg).astype(BF16)
-            gain_acc[rows, :] += pg * m2
-
-    def step(u0, width):
-        us = pl.ds(u0, CH)
-        stem_s[...] = dot(wcat[...], oh[:, us])
-        ag_s[:, 0:width] = dot(wt[...], gt[:, pl.ds(u0, width)])
-
-        def chunk(i, _):
-            r0 = pl.multiple_of(i * 16, 16)
-            rows = pl.ds(r0, 16)
-            rows2 = pl.ds(pl.multiple_of(C1 + r0, 16), 16)
-            for lt in range(2):
-                tile(0, lt, rows, rows2, u0, lt * 128 < width)
-            return 0
-
-        lax.fori_loop(0, C1 // 16, chunk, 0, unroll=2)
-        stem_acc[...] += dot_nt(sg_s[:, 0:width], oh[:, pl.ds(u0, width)])
-
-    def group(g, _):
-        step(pl.multiple_of(g * CH, CH), CH)
-        return 0
-
-    lax.fori_loop(0, 7, group, 0)
-    step(7 * CH, 128)
-
-
-def shift_act(act, xt):
-    def rows(i, _):
-        r0 = pl.multiple_of(i * 16, 16)
-        full = act[pl.ds(r0, 16), :]
-        for t in range(K2):
-            s = t - 2
-            v = full if s == 0 else pltpu.roll(full, (-s) % WIDE, 1)
-            xt[pl.ds(pl.multiple_of(t * C1 + r0, 16), 16), :] = v[:, 0:ROWS]
-        return 0
-
-    lax.fori_loop(0, C1 // 16, rows, 0)
-
-
-def tower_part(cot_v, xt, tg_s, unit_s):
-    def tap(t, _):
-        tg_s[...] = dot_nt(cot_v[...], xt[pl.ds(pl.multiple_of(t * C1, C1), C1), :])
-        for d in range(16):
-            for ct in range(4):
-                piece = tg_s[38 * d : 38 * d + 38, ct * 128 : (ct + 1) * 128]
-                unit_s[d, pl.ds(152 * t + 38 * ct, 38), :] = piece
-        return 0
-
-    lax.fori_loop(0, K2, tap, 0)
+def pool(hd, mean, gain2):
+    gd = gain2 * hd
+    t = jnp.tanh(gd)
+    hx = mean + t * hd
+    h2 = hx * hx
+    th = jnp.tanh(hx * (2 * GELU_A + (8 * GELU_A * GELU_B) * h2))
+    p1 = 1.0 + th
+    act = hx * p1
+    dgelu = p1 * (0.25 + hx * (2.0 - p1) * (0.5 * GELU_A + (6 * GELU_A * GELU_B) * h2))
+    k = gd * (1.0 - t * t)
+    m1 = (1.0 + t) + k
+    return act, dgelu * m1, dgelu * (2.0 - m1), dgelu * (hd * k)
+
+
+def span(n):
+    return slice(n * CH, min((n + 1) * CH, ROWS))
+
+
+def ag_chunk(n, wt, gt, ag):
+    ag[:, span(n)] = dot(wt[...], gt[:, span(n)]).astype(BF16)
+
+
+def stem_chunk(n, wcat, oh, stem_s):
+    stem_s[n % 2] = dot(wcat[...], oh[:, n * CH : (n + 1) * CH])
+
+
+def pool_chunk(n, seq, stem_s, gain_b, act, fac):
+    for r in range(0, C1, 16):
+        for lt in range(2):
+            cols = slice(lt * 128, lt * 128 + 128)
+            at = slice(n * CH + lt * 128, n * CH + lt * 128 + 128)
+            a, f1, f2, f3 = pool(
+                stem_s[n % 2, r : r + 16, cols], stem_s[n % 2, C1 + r : C1 + r + 16, cols], gain_b[r : r + 16, :]
+            )
+            if at.start >= ROWS:
+                lane = lax.broadcasted_iota(I32, (16, 128), 1)
+                out = ((lane < 64) & (seq == SEQ - 1)) | ((lane >= 64) & (seq == 0))
+                a = jnp.where(out, 0.0, a)
+            else:
+                fac[0, r : r + 16, at] = f1.astype(BF16)
+                fac[1, r : r + 16, at] = f2.astype(BF16)
+                fac[2, r : r + 16, at] = f3.astype(BF16)
+            act[r : r + 16, at] = a.astype(BF16)
+
+
+def back_chunk(n, ag, fac, sg_s, gain_acc):
+    for r in range(0, C1, 16):
+        for c0 in range(span(n).start, span(n).stop, 128):
+            rs, cs = slice(r, r + 16), slice(c0, c0 + 128)
+            o = slice(c0 % CH, c0 % CH + 128)
+            g = ag[rs, cs]
+            sg_s[n % 2, rs, o] = g * fac[0, rs, cs]
+            sg_s[n % 2, C1 + r : C1 + r + 16, o] = g * fac[1, rs, cs]
+            gain_acc[rs, :] += g.astype(F32) * fac[2, rs, cs].astype(F32)
+
+
+def stem_grad_chunk(n, sg_s, oh, stem_acc):
+    w = span(n).stop - span(n).start
+    stem_acc[...] += dot_nt(sg_s[n % 2, :, 0:w], oh[0:64, span(n)])
+
+
+def shift_act(t, act, xt):
+    s = t - 2
+    for r in range(0, C1, 16):
+        v = pltpu.roll(act[r : r + 16, :], (-s) % WIDE, 1)
+        xt[t - t // 3, r : r + 16, :] = v[:, 0:ROWS]
+
+
+TAPS = (2, 1, 3, 0, 4)
+
+
+def tower_tap(i, cot_v, act, xt, tg_s, unit_s):
+    t = TAPS[i]
+    rhs = act[:, 0:ROWS] if t == 2 else xt[t - t // 3]
+    tg_s[i % 2] = dot_nt(cot_v[...], rhs)
     for d in range(16):
-        unit_s[d, 760:768, :] = jnp.zeros((8, 128), F32)
-
-
-def response_step(xt, w5, resp_v, u0, width):
+        for ct in range(4):
+            piece = tg_s[i % 2, 38 * d : 38 * d + 38, ct * 128 : (ct + 1) * 128]
+            unit_s[d, 152 * i + 38 * ct : 152 * i + 38 * ct + 38, :] = piece
+
+
+def resp_chunk(n, w5, act, xt, resp_v):
+    cols = span(n)
     taps = jnp.concatenate([w5[t] for t in range(K2)], axis=1)
-    cols = pl.ds(u0, width)
-    resp_v[:, cols] = dot(taps, xt[:, cols]).astype(BF16)
+    rhs = jnp.concatenate([act[:, cols] if t == 2 else xt[t - t // 3, :, cols] for t in range(K2)], axis=0)
+    resp_v[:, cols] = dot(taps, rhs).astype(BF16)
 
 
 ORDER = ((0, 1, 2), (1, 2, 0), (2, 0, 1))
@@ -338,22 +343,23 @@
         for p in range(3):
             r0 = p * 256 + (s % 4) * 64 + (s // 4) * 32
             flat[r0 : r0 + 32, :] = gath[s, p].astype(F32)
-    for t in range(K2):
+    for i, t in enumerate(TAPS):
         for ct in range(4):
-            j = 4 * t + ct
+            j = 4 * i + ct
             tower_ref[t, :, ct * 128 : (ct + 1) * 128] = flat[38 * j : 38 * j + 38, :]
 
 
-def pack_stem(stem_acc, gain_acc, stb):
+def pack_stem(stem_acc, gain_acc, gain, stb):
     even = stem_acc[0:C1, :]
-    odd = pltpu.roll(stem_acc[C1:, :], 60, 1) if False else jnp.concatenate(
-        [stem_acc[C1:, 4:64], stem_acc[C1:, 0:4]], axis=1
-    )
+    odd = jnp.concatenate([stem_acc[C1:, 4:64], stem_acc[C1:, 0:4]], axis=1)
     lane = lax.broadcasted_iota(I32, (C1, 64), 1)
-    gain = jnp.sum(gain_acc[...], axis=1, keepdims=True)
-    both = jnp.where(lane < 60, even + odd, jnp.where(lane == 60, gain, 0.0)).T
+    total = jnp.sum(gain_acc[...], axis=1, keepdims=True)
+    both = jnp.where(lane < 60, even + odd, jnp.where(lane == 60, total, 0.0)).T
+    row = lax.broadcasted_iota(I32, (8, 1), 0)
+    last = jnp.where(row == 4, both[56:64] * (4.0 / gain[...]), both[56:64])
     for i in range(16):
-        stb[i] = both[(i % 8) * 8 : (i % 8) * 8 + 8, (i // 8) * 256 : (i // 8) * 256 + 256]
+        cols = slice((i // 8) * 256, (i // 8) * 256 + 256)
+        stb[i] = last[:, cols] if i % 8 == 7 else both[(i % 8) * 8 : (i % 8) * 8 + 8, cols]
 
 
 def stem_plane_copies(me, src_of, recv, slot_of, ss, rs):
@@ -399,7 +405,7 @@
     packed, rc_ref, sh_ref, cot_hbm, sw_ref, gain, w_hbm,
     resp_hbm, stem_ref, gain_ref, tower_ref,
     cot_v, w5, sw_f, wcat, gain_b, wt, gt, oh, act, xt,
-    stem_s, ag_s, sg_s, gain_acc, stem_acc, resp_v, tg_s, unit_s,
+    stem_s, ag, fac, sg_s, gain_acc, stem_acc, tg_s, unit_s,
     words, halo, own, oth, recv_d, recv_1, buf_2, recv_2, fin, gath, flat,
     stb, recv_a, piece_a, recv_b, piece_b, gath_a,
     sems, ws, wr, hs, hr, ds, dr, s1, r1, s2, r2, s3, r3, sa, ra, sb, rb, sg, rg,
@@ -415,39 +421,75 @@
     edges = edge_copies(dp, seq, packed, cot_hbm, words, halo, ws, wr, hs, hr)
     start(edges)
     words[seq] = packed[...]
+    gain_acc[...] = jnp.zeros_like(gain_acc)
+    stem_acc[...] = jnp.zeros_like(stem_acc)
+    unit_s[:, 760:768, :] = jnp.zeros((16, 8, 128), F32)
     prep_stem_weight(sw_ref, sw_f, wcat, gain, gain_b)
+    c1.wait()
+    prep_cot(cot_v, gt)
     c2.wait()
     prep_tower_weight(w5, wt)
+    ag_chunk(1, wt, gt, ag)
     wait(edges)
     decode(words, rc_ref[0], sh_ref[0], seq, oh)
-    c1.wait()
-    prep_cot(cot_v, halo, seq, gt)
-    main_loop(oh, wcat, gain_b, seq, gt, wt, stem_s, ag_s, sg_s, act, gain_acc, stem_acc)
-    pack_stem(stem_acc, gain_acc, stb)
-    level_a = stem_plane_copies(me, lambda a: stb.at[a], recv_a, lambda e: e - 1, sa, ra)
-    start(level_a)
-    shift_act(act, xt)
-    tower_part(cot_v, xt, tg_s, unit_s)
-    pairs = []
-    for p in range(3):
+    rim_cot(cot_v, halo, seq, gt)
+    for n in range(8):
+        stem_chunk(n, wcat, oh, stem_s)
+        if n < 5:
+            ag_chunk(n + 2, wt, gt, ag)
+        pool_chunk(n, seq, stem_s, gain_b, act, fac)
+
+    def tap(i):
+        if i != 0:
+            shift_act(TAPS[i], act, xt)
+        tower_tap(i, cot_v, act, xt, tg_s, unit_s)
+
+    pairs, rings, planes = [], [], []
+
+    def pair(p):
         pack_part(p, me, unit_s, own, oth)
         pairs.append(pair_copy(p, me, oth, recv_d, ds, dr))
         pairs[p].start()
 
-    def resp(lo, hi):
-        def group(g, _):
-            response_step(xt, w5, resp_v, pl.multiple_of(g * CH, CH), CH)
-            return 0
-
-        lax.fori_loop(lo, hi, group, 0)
-
-    resp(0, 2)
-    rings = []
-    for p in range(3):
+    def ring(p):
         pairs[p].wait()
         pair_sum(p, own, recv_d)
         rings.append(ring_copies(p, me, own, recv_1, s1, r1))
         start(rings[p])
+
+    def plane(p):
+        wait(rings[p])
+        ring_sum(p, me, own, recv_1, buf_2)
+        planes.append(plane_copies(p, me, buf_2, recv_2, s2, r2))
+        start(planes[p])
+
+    def resp(n):
+        resp_chunk(n, w5, act, xt, cot_v)
+
+    tap(0)
+    tap(1)
+    pair(0)
+    tap(2)
+    ring(0)
+    tap(3)
+    pair(1)
+    tap(4)
+    pair(2)
+    ring(1)
+    ag_chunk(0, wt, gt, ag)
+    ag_chunk(7, wt, gt, ag)
+    ring(2)
+    for n in range(8):
+        back_chunk(n, ag, fac, sg_s, gain_acc)
+        stem_grad_chunk(n, sg_s, oh, stem_acc)
+    pack_stem(stem_acc, gain_acc, gain, stb)
+    level_a = stem_plane_copies(me, lambda a: stb.at[a], recv_a, lambda e: e - 1, sa, ra)
+    start(level_a)
+    resp(0)
+    resp(1)
+    plane(0)
+    resp(2)
+    resp(3)
     wait(level_a)
     total = stb[x * 4 + y]
     for e in range(15):
@@ -456,8 +498,9 @@
     recv_b[z * 2 + core] = total
     level_b = stem_line_copies(me, piece_a, recv_b, sb, rb)
     start(level_b)
-    resp(2, 5)
-    planes = []
+    plane(1)
+    resp(4)
+    resp(5)
     wait(level_b)
     total = recv_b[0]
     for e in range(1, 8):
@@ -466,15 +509,11 @@
     gath_a[x * 4 + y] = total
     level_c = stem_plane_copies(me, lambda a: piece_b, gath_a, lambda e: x * 4 + y, sg, rg)
     start(level_c)
-    resp(5, 7)
-    response_step(xt, w5, resp_v, 7 * CH, 128)
-    c3 = pltpu.make_async_copy(resp_v, resp_hbm, sems.at[0])
+    plane(2)
+    resp(6)
+    resp(7)
+    c3 = pltpu.make_async_copy(cot_v, resp_hbm, sems.at[0])
     c3.start()
-    for p in range(3):
-        wait(rings[p])
-        ring_sum(p, me, own, recv_1, buf_2)
-        planes.append(plane_copies(p, me, buf_2, recv_2, s2, r2))
-        start(planes[p])
     wait(level_c)
     place_stem(gath_a, stem_ref, gain_ref)
     for p in range(3):
@@ -494,21 +533,21 @@
     return [
         V((F2, ROWS), BF16),
         V((K2, F2, C1), BF16),
-        V((64, 2 * C1), F32),
-        V((2 * C1, 64), BF16),
+        V((128, C1), F32),
+        V((2 * C1, 128), BF16),
         V((C1, 128), F32),
         V((C1, KF), BF16),
         V((KF, ROWS), BF16),
-        V((64, WIDE), BF16),
+        V((128, WIDE), BF16),
         V((C1, WIDE), BF16),
-        V((K2 * C1, ROWS), BF16),
-        V((2 * C1, CH), F32),
-        V((C1, CH), F32),
-        V((2 * C1, CH), BF16),
+        V((K2 - 1, C1, ROWS), BF16),
+        V((2, 2 * C1, CH), F32),
+        V((C1, ROWS), BF16),
+        V((3, C1, ROWS), BF16),
+        V((2, 2 * C1, CH), BF16),
         V((C1, 128), F32),
         V((2 * C1, 64), F32),
-        V((F2, ROWS), BF16),
-        V((F2, C1), F32),
+        V((2, F2, C1), F32),
         V((16, UNIT, 128), F32),
         V((SEQ, 1, 256), I32),
         V((2, F2, 128), BF16),

time: 95 us -> 73.3 us (0.77)
  Pallas kernels: 87.6 us -> 65.9 us
    pallas_call x1, Pallas kernels: 87.6 us -> 65.9 us  [shards(): pl.pallas_call(whole_kernel, out_shape=(jax.ShapeDtypeStruct((F2, ROWS),...]
where the time goes in v1:
time: 73.3 us; the launch traced here: 73.1 us
  Pallas kernels  65.9 us (90%)
  local copies, waits for them, and re-layouts  5.27 us (7%)
  between operations  1.96 us (3%)
    pallas_call x1, Pallas kernels, shards(): pl.pallas_call(whole_kernel, out_shape=(jax.ShapeDtypeStruct((F2, ROWS),...  65.9 us
    unnamed x10, local copies, waits for them, and re-layouts  5.27 us

profile of v1, /device:TPU:0, one launch (start us, length us, event | category | flops | bytes accessed | tf_op | source)
XLA Modules:
  0.0 73.1 jit_solution(11609330466180185087)
XLA Ops:
  1.9 65.9 %shard_map.102 = (bf16[608,1920]{1,0:T(8,128)(2,1)}, f32[15,4,512]{2,1,0:T(4,128)}, f32[1,512]{1,0:T(1,128)}, f32[5,38,512]{2,1,0:T(8,128)}) custom-call(s32[1,256]{1,0:T(1,128)} %packed.1, s32[1]{0:T(128)S(6)} %copy.15.rc_ref, s32[1]{0:T(128)S(6)} %copy.16.sh_ref, bf16[608,1920]{1,0:T(8,128)(2,1)} %bitcast.11, bf16[15,4,512]{2,1,0:T(4,128)(2,1)} %sw_ref.1, ...), custom_call_target="tpu_custom_call" | custom-call | tf_op jit(solution)/shard_map/pallas_call | solution.py:579
  67.8 0.0 copy-start.1
  67.8 0.0 copy-start.2
  67.8 0.0 copy-start
  67.9 3.3 %copy.17 = bf16[1,1920,608]{1,2,0:T(8,128)(2,1)} copy(bf16[1,1920,608]{1,2,0:T(8,128)(2,1)} %bitcast.12) | data formatting | bytes 4669440
  71.1 0.0 copy-done.1
  71.1 0.6 copy.18
  71.8 0.0 copy-done.2
  71.8 0.6 copy.19
  72.4 0.0 copy-done
  72.4 0.8 %copy.20 = f32[38,5,512]{2,0,1:T(8,128)} copy(f32[38,5,512]{2,0,1:T(8,128)S(1)} %bitcast.13) | data formatting | bytes 778240
Async XLA Ops:
  67.8 3.3 %copy-start.1 = (f32[15,4,512]{2,1,0:T(4,128)S(1)}, f32[15,4,512]{2,1,0:T(4,128)}, u32[]{:S(2)}) copy-start(f32[15,4,512]{2,1,0:T(4,128)} %get-tuple-element.17) | copy-start | bytes 368644
  67.8 4.0 %copy-start.2 = (f32[1,512]{1,0:T(1,128)S(1)}, f32[1,512]{1,0:T(1,128)}, u32[]{:S(2)}) copy-start(f32[1,512]{1,0:T(1,128)} %get-tuple-element.10) | copy-start | bytes 6148
  67.8 4.5 %copy-start = (f32[5,38,512]{2,1,0:T(8,128)S(1)}, f32[5,38,512]{2,1,0:T(8,128)}, u32[]{:S(2)}) copy-start(f32[5,38,512]{2,1,0:T(8,128)} %get-tuple-element.11) | copy-start | bytes 1167364

commit v2 on v1

--- a/solution.py
+++ b/solution.py
@@ -65,14 +65,13 @@
     gt[K2 * F2 : KF, :] = jnp.zeros((KF - K2 * F2, ROWS), BF16)
 
 
-def rim_cot(cot_v, halo, seq, gt):
-    lane = lax.broadcasted_iota(I32, (16, 128), 1)
+def rim_cot(cot_v, halo, seq, rim, gt):
+    nxt = jnp.where(seq < SEQ - 1, halo[1].astype(F32), 0.0)
+    prv = jnp.where(seq > 0, halo[0].astype(F32), 0.0)
+    rim[...] = jnp.concatenate([nxt, jnp.zeros((96, F2), F32), prv], axis=0).T.astype(BF16)
     for r in range(0, F2, 16):
         rs = slice(r, r + 16)
-        nxt = jnp.where(seq < SEQ - 1, halo[1, rs, :].astype(F32), 0.0)
-        prv = jnp.where(seq > 0, halo[0, rs, :].astype(F32), 0.0)
-        rim = jnp.where(lane < 64, nxt, prv).astype(BF16)
-        ring = jnp.concatenate([cot_v[rs, ROWS - 256 : ROWS], rim, cot_v[rs, 0:256]], axis=1)
+        ring = jnp.concatenate([cot_v[rs, ROWS - 256 : ROWS], rim[rs, :], cot_v[rs, 0:256]], axis=1)
         for t in range(K2):
             s = 2 - t
             if s != 0:
@@ -251,29 +250,29 @@
     pl.semaphore_wait(barrier, len(peers))
 
 
-def edge_copies(dp, seq, packed, cot_hbm, words, halo, ws, wr, hs, hr):
-    out = []
-    for d in range(1, SEQ):
-        out.append(send(packed, words.at[seq], ws.at[d - 1], wr.at[d - 1], (dp, (seq + d) % SEQ)))
-    out.append(send(cot_hbm.at[:, ROWS - 128 : ROWS], halo.at[0], hs.at[0], hr.at[0], (dp, (seq + 1) % SEQ)))
-    out.append(send(cot_hbm.at[:, 0:128], halo.at[1], hs.at[1], hr.at[1], (dp, (seq + SEQ - 1) % SEQ)))
-    return out
+def word_copies(dp, seq, packed, words, ws, wr):
+    return [
+        send(packed, words.at[seq], ws.at[d - 1], wr.at[d - 1], (dp, (seq + d) % SEQ)) for d in range(1, SEQ)
+    ]
+
+
+def rim_copies(dp, seq, pk, halo, hs, hr):
+    return [
+        send(pk.at[0], halo.at[1], hs.at[0], hr.at[0], (dp, (seq + SEQ - 1) % SEQ)),
+        send(pk.at[1], halo.at[0], hs.at[1], hr.at[1], (dp, (seq + 1) % SEQ)),
+    ]
 
 
 def pack_part(p, me, unit_s, own, oth):
     core = me[3]
-
-    def piece(j, _):
-        at = [None] * 3
+    for j in range(64):
+        at = [0, 0, 0]
         at[ORDER[p][0]], at[ORDER[p][1]], at[ORDER[p][2]] = j // 16, (j // 4) % 4, j % 4
         x, y, z = at
         unit = (y // 2) * 8 + z * 2
-        rows = pl.ds(pl.multiple_of(p * 256 + x * 64 + (y % 2) * 32, 32), 32)
-        own[p, j] = unit_s[unit + core, rows, :].astype(BF16)
-        oth[p, j] = unit_s[unit + 1 - core, rows, :].astype(BF16)
-        return 0
-
-    lax.fori_loop(0, 64, piece, 0)
+        r0 = p * 256 + x * 64 + (y % 2) * 32
+        own[p, j] = unit_s[unit + core, r0 : r0 + 32, :].astype(BF16)
+        oth[p, j] = unit_s[unit + 1 - core, r0 : r0 + 32, :].astype(BF16)
 
 
 def pair_copy(p, me, oth, recv_d, ss, rs):
@@ -282,11 +281,8 @@
 
 
 def pair_sum(p, own, recv_d):
-    def piece(j, _):
-        own[p, j] = (own[p, j].astype(F32) + recv_d[p, j].astype(F32)).astype(BF16)
-        return 0
-
-    lax.fori_loop(0, 64, piece, 0)
+    for j in range(0, 64, 4):
+        own[p, j : j + 4] = own[p, j : j + 4] + recv_d[p, j : j + 4]
 
 
 def ring_copies(p, me, own, recv_1, ss, rs):
@@ -302,15 +298,11 @@
 
 def ring_sum(p, me, own, recv_1, buf_2):
     base = me[ORDER[p][0]] * 16
-
-    def piece(j, _):
+    for j in range(16):
         total = own[p, base + j].astype(F32)
         for d in range(3):
             total = total + recv_1[p, d, j].astype(F32)
         buf_2[p, j] = total.astype(BF16)
-        return 0
-
-    lax.fori_loop(0, 16, piece, 0)
 
 
 def plane_copies(p, me, buf_2, recv_2, ss, rs):
@@ -406,37 +398,53 @@
     resp_hbm, stem_ref, gain_ref, tower_ref,
     cot_v, w5, sw_f, wcat, gain_b, wt, gt, oh, act, xt,
     stem_s, ag, fac, sg_s, gain_acc, stem_acc, tg_s, unit_s,
-    words, halo, own, oth, recv_d, recv_1, buf_2, recv_2, fin, gath, flat,
+    words, edge, pk, halo, rim, own, oth, recv_d, recv_1, buf_2, recv_2, fin, gath, flat,
     stb, recv_a, piece_a, recv_b, piece_b, gath_a,
     sems, ws, wr, hs, hr, ds, dr, s1, r1, s2, r2, s3, r3, sa, ra, sb, rb, sg, rg,
 ):
     dp, seq = lax.axis_index("dp"), lax.axis_index("seq")
     x, y, z, core = seq % 4, (dp // 8) * 2 + seq // 4, (dp // 2) % 4, dp % 2
     me = (x, y, z, core)
-    c1 = pltpu.make_async_copy(cot_hbm, cot_v, sems.at[0])
-    c2 = pltpu.make_async_copy(w_hbm, w5, sems.at[1])
-    c1.start()
-    c2.start()
+    ends = [
+        pltpu.make_async_copy(cot_hbm.at[:, 0:128], edge.at[0], sems.at[9]),
+        pltpu.make_async_copy(cot_hbm.at[:, ROWS - 128 : ROWS], edge.at[1], sems.at[10]),
+    ]
+    cuts = (0, 160, 320, 464, F2)
+    cots = [
+        pltpu.make_async_copy(
+            cot_hbm.at[cuts[i] : cuts[i + 1], :], cot_v.at[cuts[i] : cuts[i + 1], :], sems.at[i]
+        )
+        for i in range(4)
+    ]
+    weights = [pltpu.make_async_copy(w_hbm.at[t], w5.at[t], sems.at[4 + t]) for t in range(K2)]
+    start(ends)
+    start(cots)
+    start(weights)
     greet(me)
-    edges = edge_copies(dp, seq, packed, cot_hbm, words, halo, ws, wr, hs, hr)
+    edges = word_copies(dp, seq, packed, words, ws, wr)
     start(edges)
+    for i in range(2):
+        ends[i].wait()
+        pk[i] = edge[i].T[0:16] if i == 0 else edge[i].T[112:128]
+    rims = rim_copies(dp, seq, pk, halo, hs, hr)
+    start(rims)
     words[seq] = packed[...]
     gain_acc[...] = jnp.zeros_like(gain_acc)
     stem_acc[...] = jnp.zeros_like(stem_acc)
     unit_s[:, 760:768, :] = jnp.zeros((16, 8, 128), F32)
     prep_stem_weight(sw_ref, sw_f, wcat, gain, gain_b)
-    c1.wait()
+    wait(cots)
     prep_cot(cot_v, gt)
-    c2.wait()
+    wait(weights)
     prep_tower_weight(w5, wt)
-    ag_chunk(1, wt, gt, ag)
+    for n in range(1, 4):
+        ag_chunk(n, wt, gt, ag)
     wait(edges)
     decode(words, rc_ref[0], sh_ref[0], seq, oh)
-    rim_cot(cot_v, halo, seq, gt)
     for n in range(8):
         stem_chunk(n, wcat, oh, stem_s)
-        if n < 5:
-            ag_chunk(n + 2, wt, gt, ag)
+        if n < 3:
+            ag_chunk(n + 4, wt, gt, ag)
         pool_chunk(n, seq, stem_s, gain_b, act, fac)
 
     def tap(i):
@@ -475,13 +483,15 @@
     pair(1)
     tap(4)
     pair(2)
+    wait(rims)
+    rim_cot(cot_v, halo, seq, rim, gt)
+    ag_chunk(0, wt, gt, ag)
     ring(1)
-    ag_chunk(0, wt, gt, ag)
     ag_chunk(7, wt, gt, ag)
-    ring(2)
     for n in range(8):
         back_chunk(n, ag, fac, sg_s, gain_acc)
         stem_grad_chunk(n, sg_s, oh, stem_acc)
+    ring(2)
     pack_stem(stem_acc, gain_acc, gain, stb)
     level_a = stem_plane_copies(me, lambda a: stb.at[a], recv_a, lambda e: e - 1, sa, ra)
     start(level_a)
@@ -489,7 +499,6 @@
     resp(1)
     plane(0)
     resp(2)
-    resp(3)
     wait(level_a)
     total = stb[x * 4 + y]
     for e in range(15):
@@ -498,9 +507,9 @@
     recv_b[z * 2 + core] = total
     level_b = stem_line_copies(me, piece_a, recv_b, sb, rb)
     start(level_b)
+    resp(3)
+    resp(4)
     plane(1)
-    resp(4)
-    resp(5)
     wait(level_b)
     total = recv_b[0]
     for e in range(1, 8):
@@ -509,19 +518,20 @@
     gath_a[x * 4 + y] = total
     level_c = stem_plane_copies(me, lambda a: piece_b, gath_a, lambda e: x * 4 + y, sg, rg)
     start(level_c)
+    resp(5)
+    resp(6)
     plane(2)
-    resp(6)
     resp(7)
     c3 = pltpu.make_async_copy(cot_v, resp_hbm, sems.at[0])
     c3.start()
-    wait(level_c)
-    place_stem(gath_a, stem_ref, gain_ref)
     for p in range(3):
         wait(planes[p])
         plane_sum(p, me, buf_2, recv_2, fin)
     share = share_copies(dp, seq, fin, gath, s3, r3)
     start(share)
     gath[seq] = fin[...]
+    wait(level_c)
+    place_stem(gath_a, stem_ref, gain_ref)
     c3.wait()
     wait(share)
     place_tower(gath, flat, tower_ref)
@@ -551,6 +561,9 @@
         V((16, UNIT, 128), F32),
         V((SEQ, 1, 256), I32),
         V((2, F2, 128), BF16),
+        V((2, 16, F2), BF16),
+        V((2, 16, F2), BF16),
+        V((F2, 128), BF16),
         V((3, 64, 32, 128), BF16),
         V((3, 64, 32, 128), BF16),
         V((3, 64, 32, 128), BF16),
@@ -566,10 +579,22 @@
         V((8, 8, 256), F32),
         V((8, 256), F32),
         V((16, 8, 256), F32),
-        D((2,)), D((7,)), D((7,)), D((2,)), D((2,)), D((3,)), D((3,)),
+        D((11,)), D((7,)), D((7,)), D((2,)), D((2,)), D((3,)), D((3,)),
         D((3, 3)), D((3, 3)), D((3, 15)), D((3, 15)), D((7,)), D((7,)),
         D((15,)), D((15,)), D((7,)), D((7,)), D((15,)), D((15,)),
     ]
+
+
+def hand_over(resp, stem, gain, tower, resp_o, stem_o, gain_o, tower_o, sems):
+    cuts = (0, 160, 320, 464, F2)
+    copies = [
+        pltpu.make_async_copy(resp.at[cuts[i] : cuts[i + 1], :], resp_o.at[cuts[i] : cuts[i + 1], :], sems.at[i])
+        for i in range(4)
+    ]
+    for i, (src, dst) in enumerate(((stem, stem_o), (gain, gain_o), (tower, tower_o))):
+        copies.append(pltpu.make_async_copy(src, dst, sems.at[4 + i]))
+    start(copies)
+    wait(copies)
 
 
 def shards(packed, rc_flags, shifts, cotangent, stem_weight, pool_gain, tower_weight):
@@ -594,6 +619,13 @@
         packed, rc_flags, shifts, cotangent[0].T, stem_weight, pool_gain[None],
         jnp.transpose(tower_weight, (1, 0, 2)),
     )
+    resp, stem, gain, tower = pl.pallas_call(
+        hand_over,
+        out_shape=tuple(jax.ShapeDtypeStruct(v.shape, v.dtype) for v in (resp, stem, gain, tower)),
+        in_specs=[A] * 4,
+        out_specs=(A,) * 4,
+        scratch_shapes=[pltpu.SemaphoreType.DMA((7,))],
+    )(resp, stem, gain, tower)
     return resp.T[None], stem, gain[0], jnp.transpose(tower, (1, 0, 2))
 
 

time: 73.3 us -> 153 us (2.09)
  Pallas kernels: 65.9 us -> 150 us
  local copies, waits for them, and re-layouts: 5.27 us -> 0 us
    pallas_call x0 -> x1, Pallas kernels: none -> 88.1 us  [shards(): pl.pallas_call(hand_over, out_shape=tuple((jax.ShapeDtypeStruct(v.shape,...]
    unnamed x10 -> x0, local copies, waits for them, and re-layouts: 5.27 us -> none
    pallas_call x1, Pallas kernels: 65.9 us -> 62.4 us  [shards(): pl.pallas_call(whole_kernel, out_shape=(jax.ShapeDtypeStruct((F2, ROWS),...]
where the time goes in v2:
time: 153 us
  Pallas kernels  150 us (98%)
  between operations  2.11 us (1%)
    pallas_call x1, Pallas kernels, shards(): pl.pallas_call(hand_over, out_shape=tuple((jax.ShapeDtypeStruct(v.shape,...  88.1 us
    pallas_call x1, Pallas kernels, shards(): pl.pallas_call(whole_kernel, out_shape=(jax.ShapeDtypeStruct((F2, ROWS),...  62.4 us

profile of v2, /device:TPU:0, one launch (start us, length us, event | category | flops | bytes accessed | tf_op | source)
XLA Modules:
  0.0 152.6 jit_solution(8785280442187352477)
XLA Ops:
  1.9 62.4 %shard_map.102 = (bf16[608,1920]{1,0:T(8,128)(2,1)}, f32[15,4,512]{2,1,0:T(4,128)}, f32[1,512]{1,0:T(1,128)}, f32[5,38,512]{2,1,0:T(8,128)}) custom-call(s32[1,256]{1,0:T(1,128)} %packed.1, s32[1]{0:T(128)S(6)} %copy.11.rc_ref, s32[1]{0:T(128)S(6)} %copy.12.sh_ref, bf16[608,1920]{1,0:T(8,128)(2,1)} %bitcast.11, bf16[15,4,512]{2,1,0:T(4,128)(2,1)} %sw_ref.1, ...), custom_call_target="tpu_custom_call" | custom-call | tf_op jit(solution)/shard_map/pallas_call | solution.py:604
  64.3 88.1 %shard_map.103 = (bf16[608,1920]{1,0:T(8,128)(2,1)}, f32[15,4,512]{2,1,0:T(4,128)}, f32[1,512]{1,0:T(1,128)}, f32[5,38,512]{2,1,0:T(8,128)}) custom-call(bf16[608,1920]{1,0:T(8,128)(2,1)} %get-tuple-element.12.resp, f32[15,4,512]{2,1,0:T(4,128)} %get-tuple-element.13.stem, f32[1,512]{1,0:T(1,128)} %get-tuple-element.14.gain, ...), custom_call_target="tpu_custom_call" | custom-call | tf_op jit(solution)/shard_map/pallas_call | solution.py:622

commit v3 on v2

--- a/solution.py
+++ b/solution.py
@@ -483,22 +483,26 @@
     pair(1)
     tap(4)
     pair(2)
+    ring(1)
     wait(rims)
     rim_cot(cot_v, halo, seq, rim, gt)
     ag_chunk(0, wt, gt, ag)
-    ring(1)
+    ring(2)
     ag_chunk(7, wt, gt, ag)
     for n in range(8):
         back_chunk(n, ag, fac, sg_s, gain_acc)
         stem_grad_chunk(n, sg_s, oh, stem_acc)
-    ring(2)
     pack_stem(stem_acc, gain_acc, gain, stb)
     level_a = stem_plane_copies(me, lambda a: stb.at[a], recv_a, lambda e: e - 1, sa, ra)
     start(level_a)
     resp(0)
     resp(1)
+    resp(2)
     plane(0)
-    resp(2)
+    resp(3)
+    resp(4)
+    resp(5)
+    plane(1)
     wait(level_a)
     total = stb[x * 4 + y]
     for e in range(15):
@@ -507,9 +511,11 @@
     recv_b[z * 2 + core] = total
     level_b = stem_line_copies(me, piece_a, recv_b, sb, rb)
     start(level_b)
-    resp(3)
-    resp(4)
-    plane(1)
+    resp(6)
+    plane(2)
+    resp(7)
+    c3 = pltpu.make_async_copy(cot_v, resp_hbm, sems.at[0])
+    c3.start()
     wait(level_b)
     total = recv_b[0]
     for e in range(1, 8):
@@ -518,12 +524,6 @@
     gath_a[x * 4 + y] = total
     level_c = stem_plane_copies(me, lambda a: piece_b, gath_a, lambda e: x * 4 + y, sg, rg)
     start(level_c)
-    resp(5)
-    resp(6)
-    plane(2)
-    resp(7)
-    c3 = pltpu.make_async_copy(cot_v, resp_hbm, sems.at[0])
-    c3.start()
     for p in range(3):
         wait(planes[p])
         plane_sum(p, me, buf_2, recv_2, fin)
@@ -585,16 +585,21 @@
     ]
 
 
-def hand_over(resp, stem, gain, tower, resp_o, stem_o, gain_o, tower_o, sems):
-    cuts = (0, 160, 320, 464, F2)
-    copies = [
-        pltpu.make_async_copy(resp.at[cuts[i] : cuts[i + 1], :], resp_o.at[cuts[i] : cuts[i + 1], :], sems.at[i])
-        for i in range(4)
-    ]
-    for i, (src, dst) in enumerate(((stem, stem_o), (gain, gain_o), (tower, tower_o))):
-        copies.append(pltpu.make_async_copy(src, dst, sems.at[4 + i]))
-    start(copies)
-    wait(copies)
+CUTS = (0, 80, 160, 240, 320, 400, 480, 544, F2)
+
+
+def hand_over(resp, stem, gain, tower, resp_o, stem_o, gain_o, tower_o, resp_v, stem_v, gain_v, tower_v, si, so):
+    way = [(stem, stem_v, stem_o), (gain, gain_v, gain_o), (tower, tower_v, tower_o)]
+    for i in range(8):
+        rows = slice(CUTS[i], CUTS[i + 1])
+        way.append((resp.at[rows, :], resp_v.at[rows, :], resp_o.at[rows, :]))
+    into = [pltpu.make_async_copy(w[0], w[1], si.at[i]) for i, w in enumerate(way)]
+    out = [pltpu.make_async_copy(w[1], w[2], so.at[i]) for i, w in enumerate(way)]
+    start(into)
+    for i in range(len(way)):
+        into[i].wait()
+        out[i].start()
+    wait(out)
 
 
 def shards(packed, rc_flags, shifts, cotangent, stem_weight, pool_gain, tower_weight):
@@ -624,7 +629,15 @@
         out_shape=tuple(jax.ShapeDtypeStruct(v.shape, v.dtype) for v in (resp, stem, gain, tower)),
         in_specs=[A] * 4,
         out_specs=(A,) * 4,
-        scratch_shapes=[pltpu.SemaphoreType.DMA((7,))],
+        scratch_shapes=[
+            pltpu.VMEM((F2, ROWS), BF16),
+            pltpu.VMEM((K1, 4, C1), F32),
+            pltpu.VMEM((1, C1), F32),
+            pltpu.VMEM((K2, 38, C1), F32),
+            pltpu.SemaphoreType.DMA((11,)),
+            pltpu.SemaphoreType.DMA((11,)),
+        ],
+        compiler_params=pltpu.CompilerParams(vmem_limit_bytes=60 * 1024 * 1024),
     )(resp, stem, gain, tower)
     return resp.T[None], stem, gain[0], jnp.transpose(tower, (1, 0, 2))
 

time: 153 us -> 65.2 us (0.43)
  Pallas kernels: 150 us -> 62.7 us
    pallas_call x1, Pallas kernels: 88.1 us -> 2.78 us  [shards(): pl.pallas_call(hand_over, out_shape=tuple((jax.ShapeDtypeStruct(v.shape,...]
    pallas_call x1, Pallas kernels: 62.4 us -> 59.9 us  [shards(): pl.pallas_call(whole_kernel, out_shape=(jax.ShapeDtypeStruct((F2, ROWS),...]
where the time goes in v3:
time: 65.2 us; the launch traced here: 64.8 us
  Pallas kernels  62.7 us (96%)
  between operations  2.11 us (3%)
    pallas_call x1, Pallas kernels, shards(): pl.pallas_call(whole_kernel, out_shape=(jax.ShapeDtypeStruct((F2, ROWS),...  59.9 us
    pallas_call x1, Pallas kernels, shards(): pl.pallas_call(hand_over, out_shape=tuple((jax.ShapeDtypeStruct(v.shape,...  2.78 us

profile of v3, /device:TPU:0, one launch (start us, length us, event | category | flops | bytes accessed | tf_op | source)
XLA Modules:
  0.0 64.8 jit_solution(15262666931987021655)
XLA Ops:
  1.9 59.9 %shard_map.102 = (bf16[608,1920]{1,0:T(8,128)(2,1)}, f32[15,4,512]{2,1,0:T(4,128)}, f32[1,512]{1,0:T(1,128)}, f32[5,38,512]{2,1,0:T(8,128)}) custom-call(s32[1,256]{1,0:T(1,128)} %packed.1, s32[1]{0:T(128)S(6)} %copy.11.rc_ref, s32[1]{0:T(128)S(6)} %copy.12.sh_ref, bf16[608,1920]{1,0:T(8,128)(2,1)} %bitcast.11, bf16[15,4,512]{2,1,0:T(4,128)(2,1)} %sw_ref.1, ...), custom_call_target="tpu_custom_call" | custom-call | tf_op jit(solution)/shard_map/pallas_call | solution.py:609
  61.9 2.8 %shard_map.103 = (bf16[608,1920]{1,0:T(8,128)(2,1)}, f32[15,4,512]{2,1,0:T(4,128)}, f32[1,512]{1,0:T(1,128)}, f32[5,38,512]{2,1,0:T(8,128)}) custom-call(bf16[608,1920]{1,0:T(8,128)(2,1)} %get-tuple-element.12.resp, f32[15,4,512]{2,1,0:T(4,128)} %get-tuple-element.13.stem, f32[1,512]{1,0:T(1,128)} %get-tuple-element.14.gain, ...), custom_call_target="tpu_custom_call" | custom-call | tf_op jit(solution)/shard_map/pallas_call | solution.py:627

commit v4 on v3

--- a/solution.py
+++ b/solution.py
@@ -132,18 +132,22 @@
 GELU_B = 0.044715
 
 
-def pool(hd, mean, gain2):
+def activate(hd, mean, gain2):
+    hx = mean + jnp.tanh(gain2 * hd) * hd
+    th = jnp.tanh(hx * (2 * GELU_A + (8 * GELU_A * GELU_B) * (hx * hx)))
+    return hx * (1.0 + th)
+
+
+def factors(hd, mean, gain2):
     gd = gain2 * hd
     t = jnp.tanh(gd)
     hx = mean + t * hd
     h2 = hx * hx
-    th = jnp.tanh(hx * (2 * GELU_A + (8 * GELU_A * GELU_B) * h2))
-    p1 = 1.0 + th
-    act = hx * p1
+    p1 = 1.0 + jnp.tanh(hx * (2 * GELU_A + (8 * GELU_A * GELU_B) * h2))
     dgelu = p1 * (0.25 + hx * (2.0 - p1) * (0.5 * GELU_A + (6 * GELU_A * GELU_B) * h2))
     k = gd * (1.0 - t * t)
     m1 = (1.0 + t) + k
-    return act, dgelu * m1, dgelu * (2.0 - m1), dgelu * (hd * k)
+    return dgelu * m1, dgelu * (2.0 - m1), dgelu * (hd * k)
 
 
 def span(n):
@@ -158,23 +162,30 @@
     stem_s[n % 2] = dot(wcat[...], oh[:, n * CH : (n + 1) * CH])
 
 
-def pool_chunk(n, seq, stem_s, gain_b, act, fac):
+def act_chunk(n, seq, stem_s, gain_b, act):
     for r in range(0, C1, 16):
         for lt in range(2):
             cols = slice(lt * 128, lt * 128 + 128)
             at = slice(n * CH + lt * 128, n * CH + lt * 128 + 128)
-            a, f1, f2, f3 = pool(
+            a = activate(
                 stem_s[n % 2, r : r + 16, cols], stem_s[n % 2, C1 + r : C1 + r + 16, cols], gain_b[r : r + 16, :]
             )
             if at.start >= ROWS:
                 lane = lax.broadcasted_iota(I32, (16, 128), 1)
                 out = ((lane < 64) & (seq == SEQ - 1)) | ((lane >= 64) & (seq == 0))
                 a = jnp.where(out, 0.0, a)
-            else:
-                fac[0, r : r + 16, at] = f1.astype(BF16)
-                fac[1, r : r + 16, at] = f2.astype(BF16)
-                fac[2, r : r + 16, at] = f3.astype(BF16)
             act[r : r + 16, at] = a.astype(BF16)
+
+
+def factor_chunk(n, stem_s, gain_b, fac):
+    for r in range(0, C1, 16):
+        for c0 in range(span(n).start, span(n).stop, 128):
+            cols = slice(c0 % CH, c0 % CH + 128)
+            made = factors(
+                stem_s[n % 2, r : r + 16, cols], stem_s[n % 2, C1 + r : C1 + r + 16, cols], gain_b[r : r + 16, :]
+            )
+            for i in range(3):
+                fac[i, r : r + 16, c0 : c0 + 128] = made[i].astype(BF16)
 
 
 def back_chunk(n, ag, fac, sg_s, gain_acc):
@@ -263,30 +274,33 @@
     ]
 
 
-def pack_part(p, me, unit_s, own, oth):
+def pack_group(g, me, unit_s, own, oth):
     core = me[3]
-    for j in range(64):
-        at = [0, 0, 0]
-        at[ORDER[p][0]], at[ORDER[p][1]], at[ORDER[p][2]] = j // 16, (j // 4) % 4, j % 4
-        x, y, z = at
-        unit = (y // 2) * 8 + z * 2
-        r0 = p * 256 + x * 64 + (y % 2) * 32
-        own[p, j] = unit_s[unit + core, r0 : r0 + 32, :].astype(BF16)
-        oth[p, j] = unit_s[unit + 1 - core, r0 : r0 + 32, :].astype(BF16)
-
-
-def pair_copy(p, me, oth, recv_d, ss, rs):
+    for p in range(3):
+        for j in range(64):
+            at = [0, 0, 0]
+            at[ORDER[p][0]], at[ORDER[p][1]], at[ORDER[p][2]] = j // 16, (j // 4) % 4, j % 4
+            x, y, z = at
+            unit = (y // 2) * 8 + z * 2
+            r0 = g * 384 + p * 128 + x * 32 + (y % 2) * 16
+            own[3 * g + p, j] = unit_s[unit + core, r0 : r0 + 16, :].astype(BF16)
+            oth[3 * g + p, j] = unit_s[unit + 1 - core, r0 : r0 + 16, :].astype(BF16)
+
+
+def pair_copy(g, me, oth, recv_d, ss, rs):
     x, y, z, core = me
-    return send(oth.at[p], recv_d.at[p], ss.at[p], rs.at[p], device_at(x, y, z, 1 - core))
-
-
-def pair_sum(p, own, recv_d):
-    for j in range(0, 64, 4):
-        own[p, j : j + 4] = own[p, j : j + 4] + recv_d[p, j : j + 4]
+    part = pl.ds(3 * g, 3)
+    return send(oth.at[part], recv_d.at[part], ss.at[g], rs.at[g], device_at(x, y, z, 1 - core))
+
+
+def pair_sum(g, own, recv_d):
+    for p in range(3 * g, 3 * g + 3):
+        for j in range(0, 64, 8):
+            own[p, j : j + 8] = own[p, j : j + 8] + recv_d[p, j : j + 8]
 
 
 def ring_copies(p, me, own, recv_1, ss, rs):
-    axis = ORDER[p][0]
+    axis = ORDER[p % 3][0]
     out = []
     for d in range(1, 4):
         to = list(me)
@@ -297,7 +311,7 @@
 
 
 def ring_sum(p, me, own, recv_1, buf_2):
-    base = me[ORDER[p][0]] * 16
+    base = me[ORDER[p % 3][0]] * 16
     for j in range(16):
         total = own[p, base + j].astype(F32)
         for d in range(3):
@@ -306,7 +320,7 @@
 
 
 def plane_copies(p, me, buf_2, recv_2, ss, rs):
-    b, c = ORDER[p][1], ORDER[p][2]
+    b, c = ORDER[p % 3][1], ORDER[p % 3][2]
     out = []
     for e in range(1, 16):
         to = list(me)
@@ -318,7 +332,7 @@
 
 
 def plane_sum(p, me, buf_2, recv_2, fin):
-    total = buf_2[p, me[ORDER[p][1]] * 4 + me[ORDER[p][2]]].astype(F32)
+    total = buf_2[p, me[ORDER[p % 3][1]] * 4 + me[ORDER[p % 3][2]]].astype(F32)
     for e in range(15):
         total = total + recv_2[p, e].astype(F32)
     fin[p] = total.astype(BF16)
@@ -332,9 +346,9 @@
 
 def place_tower(gath, flat, tower_ref):
     for s in range(SEQ):
-        for p in range(3):
-            r0 = p * 256 + (s % 4) * 64 + (s // 4) * 32
-            flat[r0 : r0 + 32, :] = gath[s, p].astype(F32)
+        for p in range(6):
+            r0 = p * 128 + (s % 4) * 32 + (s // 4) * 16
+            flat[r0 : r0 + 16, :] = gath[s, p].astype(F32)
     for i, t in enumerate(TAPS):
         for ct in range(4):
             j = 4 * i + ct
@@ -443,9 +457,7 @@
     decode(words, rc_ref[0], sh_ref[0], seq, oh)
     for n in range(8):
         stem_chunk(n, wcat, oh, stem_s)
-        if n < 3:
-            ag_chunk(n + 4, wt, gt, ag)
-        pool_chunk(n, seq, stem_s, gain_b, act, fac)
+        act_chunk(n, seq, stem_s, gain_b, act)
 
     def tap(i):
         if i != 0:
@@ -454,55 +466,65 @@
 
     pairs, rings, planes = [], [], []
 
-    def pair(p):
-        pack_part(p, me, unit_s, own, oth)
-        pairs.append(pair_copy(p, me, oth, recv_d, ds, dr))
-        pairs[p].start()
-
-    def ring(p):
-        pairs[p].wait()
-        pair_sum(p, own, recv_d)
-        rings.append(ring_copies(p, me, own, recv_1, s1, r1))
-        start(rings[p])
-
-    def plane(p):
-        wait(rings[p])
-        ring_sum(p, me, own, recv_1, buf_2)
-        planes.append(plane_copies(p, me, buf_2, recv_2, s2, r2))
-        start(planes[p])
+    def pair(g):
+        pack_group(g, me, unit_s, own, oth)
+        pairs.append(pair_copy(g, me, oth, recv_d, ds, dr))
+        pairs[g].start()
+
+    def ring(g):
+        pairs[g].wait()
+        pair_sum(g, own, recv_d)
+        for p in range(3 * g, 3 * g + 3):
+            rings.append(ring_copies(p, me, own, recv_1, s1, r1))
+            start(rings[p])
+
+    def plane(g):
+        for p in range(3 * g, 3 * g + 3):
+            wait(rings[p])
+            ring_sum(p, me, own, recv_1, buf_2)
+            planes.append(plane_copies(p, me, buf_2, recv_2, s2, r2))
+            start(planes[p])
+
+    def factor(*chunks):
+        for n in chunks:
+            stem_chunk(n, wcat, oh, stem_s)
+            factor_chunk(n, stem_s, gain_b, fac)
 
     def resp(n):
         resp_chunk(n, w5, act, xt, cot_v)
 
     tap(0)
+    factor(0)
     tap(1)
+    factor(1, 2)
+    tap(2)
     pair(0)
-    tap(2)
+    factor(3, 4)
+    tap(3)
     ring(0)
-    tap(3)
+    factor(5, 6)
+    tap(4)
     pair(1)
-    tap(4)
-    pair(2)
-    ring(1)
+    factor(7)
     wait(rims)
     rim_cot(cot_v, halo, seq, rim, gt)
-    ag_chunk(0, wt, gt, ag)
-    ring(2)
-    ag_chunk(7, wt, gt, ag)
+    ag_chunk(4, wt, gt, ag)
+    ring(1)
+    for n in (5, 6, 0, 7):
+        ag_chunk(n, wt, gt, ag)
     for n in range(8):
         back_chunk(n, ag, fac, sg_s, gain_acc)
         stem_grad_chunk(n, sg_s, oh, stem_acc)
     pack_stem(stem_acc, gain_acc, gain, stb)
     level_a = stem_plane_copies(me, lambda a: stb.at[a], recv_a, lambda e: e - 1, sa, ra)
     start(level_a)
+    plane(0)
     resp(0)
     resp(1)
     resp(2)
-    plane(0)
+    plane(1)
     resp(3)
     resp(4)
-    resp(5)
-    plane(1)
     wait(level_a)
     total = stb[x * 4 + y]
     for e in range(15):
@@ -511,11 +533,17 @@
     recv_b[z * 2 + core] = total
     level_b = stem_line_copies(me, piece_a, recv_b, sb, rb)
     start(level_b)
+    resp(5)
     resp(6)
-    plane(2)
     resp(7)
     c3 = pltpu.make_async_copy(cot_v, resp_hbm, sems.at[0])
     c3.start()
+    for p in range(6):
+        wait(planes[p])
+        plane_sum(p, me, buf_2, recv_2, fin)
+    share = share_copies(dp, seq, fin, gath, s3, r3)
+    start(share)
+    gath[seq] = fin[...]
     wait(level_b)
     total = recv_b[0]
     for e in range(1, 8):
@@ -524,17 +552,11 @@
     gath_a[x * 4 + y] = total
     level_c = stem_plane_copies(me, lambda a: piece_b, gath_a, lambda e: x * 4 + y, sg, rg)
     start(level_c)
-    for p in range(3):
-        wait(planes[p])
-        plane_sum(p, me, buf_2, recv_2, fin)
-    share = share_copies(dp, seq, fin, gath, s3, r3)
-    start(share)
-    gath[seq] = fin[...]
-    wait(level_c)
-    place_stem(gath_a, stem_ref, gain_ref)
     c3.wait()
     wait(share)
     place_tower(gath, flat, tower_ref)
+    wait(level_c)
+    place_stem(gath_a, stem_ref, gain_ref)
 
 
 def scratch():
@@ -564,14 +586,14 @@
         V((2, 16, F2), BF16),
         V((2, 16, F2), BF16),
         V((F2, 128), BF16),
-        V((3, 64, 32, 128), BF16),
-        V((3, 64, 32, 128), BF16),
-        V((3, 64, 32, 128), BF16),
-        V((3, 3, 16, 32, 128), BF16),
-        V((3, 16, 32, 128), BF16),
-        V((3, 15, 32, 128), BF16),
-        V((3, 32, 128), BF16),
-        V((SEQ, 3, 32, 128), BF16),
+        V((6, 64, 16, 128), BF16),
+        V((6, 64, 16, 128), BF16),
+        V((6, 64, 16, 128), BF16),
+        V((6, 3, 16, 16, 128), BF16),
+        V((6, 16, 16, 128), BF16),
+        V((6, 15, 16, 128), BF16),
+        V((6, 16, 128), BF16),
+        V((SEQ, 6, 16, 128), BF16),
         V((UNIT, 128), F32),
         V((16, 8, 256), F32),
         V((15, 8, 256), F32),
@@ -579,8 +601,8 @@
         V((8, 8, 256), F32),
         V((8, 256), F32),
         V((16, 8, 256), F32),
-        D((11,)), D((7,)), D((7,)), D((2,)), D((2,)), D((3,)), D((3,)),
-        D((3, 3)), D((3, 3)), D((3, 15)), D((3, 15)), D((7,)), D((7,)),
+        D((11,)), D((7,)), D((7,)), D((2,)), D((2,)), D((2,)), D((2,)),
+        D((6, 3)), D((6, 3)), D((6, 15)), D((6, 15)), D((7,)), D((7,)),
         D((15,)), D((15,)), D((7,)), D((7,)), D((15,)), D((15,)),
     ]
 

time: 65.2 us -> 64.9 us (level)
  no operation moved by 1% of the time
where the time goes in v4:
time: 64.9 us; the launch traced here: 64.6 us
  Pallas kernels  62.5 us (96%)
  between operations  2.11 us (3%)
    pallas_call x1, Pallas kernels, shards(): pl.pallas_call(whole_kernel, out_shape=(jax.ShapeDtypeStruct((F2, ROWS),...  59.7 us
    pallas_call x1, Pallas kernels, shards(): pl.pallas_call(hand_over, out_shape=tuple((jax.ShapeDtypeStruct(v.shape,...  2.78 us

profile of v4, /device:TPU:0, one launch (start us, length us, event | category | flops | bytes accessed | tf_op | source)
XLA Modules:
  0.0 64.6 jit_solution(15117326500848923987)
XLA Ops:
  1.9 59.7 %shard_map.102 = (bf16[608,1920]{1,0:T(8,128)(2,1)}, f32[15,4,512]{2,1,0:T(4,128)}, f32[1,512]{1,0:T(1,128)}, f32[5,38,512]{2,1,0:T(8,128)}) custom-call(s32[1,256]{1,0:T(1,128)} %packed.1, s32[1]{0:T(128)S(6)} %copy.11.rc_ref, s32[1]{0:T(128)S(6)} %copy.12.sh_ref, bf16[608,1920]{1,0:T(8,128)(2,1)} %bitcast.11, bf16[15,4,512]{2,1,0:T(4,128)(2,1)} %sw_ref.1, ...), custom_call_target="tpu_custom_call" | custom-call | tf_op jit(solution)/shard_map/pallas_call | solution.py:631
  61.6 2.8 %shard_map.103 = (bf16[608,1920]{1,0:T(8,128)(2,1)}, f32[15,4,512]{2,1,0:T(4,128)}, f32[1,512]{1,0:T(1,128)}, f32[5,38,512]{2,1,0:T(8,128)}) custom-call(bf16[608,1920]{1,0:T(8,128)(2,1)} %get-tuple-element.12.resp, f32[15,4,512]{2,1,0:T(4,128)} %get-tuple-element.13.stem, f32[1,512]{1,0:T(1,128)} %get-tuple-element.14.gain, ...), custom_call_target="tpu_custom_call" | custom-call | tf_op jit(solution)/shard_map/pallas_call | solution.py:649

commit v5 on v4

--- a/solution.py
+++ b/solution.py
@@ -316,7 +316,7 @@
         total = own[p, base + j].astype(F32)
         for d in range(3):
             total = total + recv_1[p, d, j].astype(F32)
-        buf_2[p, j] = total.astype(BF16)
+        buf_2[p % 3, j, p // 3] = total.astype(BF16)
 
 
 def plane_copies(p, me, buf_2, recv_2, ss, rs):
@@ -332,10 +332,11 @@
 
 
 def plane_sum(p, me, buf_2, recv_2, fin):
-    total = buf_2[p, me[ORDER[p % 3][1]] * 4 + me[ORDER[p % 3][2]]].astype(F32)
+    total = buf_2[p, me[ORDER[p][1]] * 4 + me[ORDER[p][2]]].astype(F32)
     for e in range(15):
         total = total + recv_2[p, e].astype(F32)
-    fin[p] = total.astype(BF16)
+    for g in range(2):
+        fin[3 * g + p] = total[g].astype(BF16)
 
 
 def share_copies(dp, seq, fin, gath, ss, rs):
@@ -478,12 +479,14 @@
             rings.append(ring_copies(p, me, own, recv_1, s1, r1))
             start(rings[p])
 
-    def plane(g):
+    def ring_end(g):
         for p in range(3 * g, 3 * g + 3):
             wait(rings[p])
             ring_sum(p, me, own, recv_1, buf_2)
-            planes.append(plane_copies(p, me, buf_2, recv_2, s2, r2))
-            start(planes[p])
+
+    def plane(p):
+        planes.append(plane_copies(p, me, buf_2, recv_2, s2, r2))
+        start(planes[p])
 
     def factor(*chunks):
         for n in chunks:
@@ -518,13 +521,13 @@
     pack_stem(stem_acc, gain_acc, gain, stb)
     level_a = stem_plane_copies(me, lambda a: stb.at[a], recv_a, lambda e: e - 1, sa, ra)
     start(level_a)
-    plane(0)
+    ring_end(0)
     resp(0)
     resp(1)
     resp(2)
-    plane(1)
-    resp(3)
-    resp(4)
+    ring_end(1)
+    for p in range(3):
+        plane(p)
     wait(level_a)
     total = stb[x * 4 + y]
     for e in range(15):
@@ -533,12 +536,11 @@
     recv_b[z * 2 + core] = total
     level_b = stem_line_copies(me, piece_a, recv_b, sb, rb)
     start(level_b)
+    resp(3)
+    resp(4)
     resp(5)
     resp(6)
-    resp(7)
-    c3 = pltpu.make_async_copy(cot_v, resp_hbm, sems.at[0])
-    c3.start()
-    for p in range(6):
+    for p in range(3):
         wait(planes[p])
         plane_sum(p, me, buf_2, recv_2, fin)
     share = share_copies(dp, seq, fin, gath, s3, r3)
@@ -552,6 +554,9 @@
     gath_a[x * 4 + y] = total
     level_c = stem_plane_copies(me, lambda a: piece_b, gath_a, lambda e: x * 4 + y, sg, rg)
     start(level_c)
+    resp(7)
+    c3 = pltpu.make_async_copy(cot_v, resp_hbm, sems.at[0])
+    c3.start()
     c3.wait()
     wait(share)
     place_tower(gath, flat, tower_ref)
@@ -590,8 +595,8 @@
         V((6, 64, 16, 128), BF16),
         V((6, 64, 16, 128), BF16),
         V((6, 3, 16, 16, 128), BF16),
-        V((6, 16, 16, 128), BF16),
-        V((6, 15, 16, 128), BF16),
+        V((3, 16, 2, 16, 128), BF16),
+        V((3, 15, 2, 16, 128), BF16),
         V((6, 16, 128), BF16),
         V((SEQ, 6, 16, 128), BF16),
         V((UNIT, 128), F32),
@@ -602,7 +607,7 @@
         V((8, 256), F32),
         V((16, 8, 256), F32),
         D((11,)), D((7,)), D((7,)), D((2,)), D((2,)), D((2,)), D((2,)),
-        D((6, 3)), D((6, 3)), D((6, 15)), D((6, 15)), D((7,)), D((7,)),
+        D((6, 3)), D((6, 3)), D((3, 15)), D((3, 15)), D((7,)), D((7,)),
         D((15,)), D((15,)), D((7,)), D((7,)), D((15,)), D((15,)),
     ]
 

time: 64.9 us -> 63.8 us (0.983)
  Pallas kernels: 62.5 us -> 61.5 us
    pallas_call x1, Pallas kernels: 59.7 us -> 58.7 us  [shards(): pl.pallas_call(whole_kernel, out_shape=(jax.ShapeDtypeStruct((F2, ROWS),...]
where the time goes in v5:
time: 63.8 us; the launch traced here: 63.6 us
  Pallas kernels  61.5 us (96%)
  between operations  2.11 us (3%)
    pallas_call x1, Pallas kernels, shards(): pl.pallas_call(whole_kernel, out_shape=(jax.ShapeDtypeStruct((F2, ROWS),...  58.7 us
    pallas_call x1, Pallas kernels, shards(): pl.pallas_call(hand_over, out_shape=tuple((jax.ShapeDtypeStruct(v.shape,...  2.78 us

profile of v5, /device:TPU:0, one launch (start us, length us, event | category | flops | bytes accessed | tf_op | source)
XLA Modules:
  0.0 63.6 jit_solution(4341968047666813581)
XLA Ops:
  1.9 58.7 %shard_map.102 = (bf16[608,1920]{1,0:T(8,128)(2,1)}, f32[15,4,512]{2,1,0:T(4,128)}, f32[1,512]{1,0:T(1,128)}, f32[5,38,512]{2,1,0:T(8,128)}) custom-call(s32[1,256]{1,0:T(1,128)} %packed.1, s32[1]{0:T(128)S(6)} %copy.11.rc_ref, s32[1]{0:T(128)S(6)} %copy.12.sh_ref, bf16[608,1920]{1,0:T(8,128)(2,1)} %bitcast.11, bf16[15,4,512]{2,1,0:T(4,128)(2,1)} %sw_ref.1, ...), custom_call_target="tpu_custom_call" | custom-call | tf_op jit(solution)/shard_map/pallas_call | solution.py:636
  60.7 2.8 %shard_map.103 = (bf16[608,1920]{1,0:T(8,128)(2,1)}, f32[15,4,512]{2,1,0:T(4,128)}, f32[1,512]{1,0:T(1,128)}, f32[5,38,512]{2,1,0:T(8,128)}) custom-call(bf16[608,1920]{1,0:T(8,128)(2,1)} %get-tuple-element.12.resp, f32[15,4,512]{2,1,0:T(4,128)} %get-tuple-element.13.stem, f32[1,512]{1,0:T(1,128)} %get-tuple-element.14.gain, ...), custom_call_target="tpu_custom_call" | custom-call | tf_op jit(solution)/shard_map/pallas_call | solution.py:654
